TPU v7x, 512 devices: a whole 4x8x8 slice. The times are simulated.
512 devices in a mesh: grp: 2 (over core), kv: 8 (over z), srv: 32 (over x, y).
Axes of the slice: x: 4, y: 8, z: 8, core: 2. Of those that a mesh axis runs over, the one named last changes fastest.
Arguments:
- queries: bfloat16 [8192, 8, 1024], P('srv', 'kv', 'grp'), may hold values from -120 to 120
- keys: bfloat16 [8192, 8, 128], P('srv', 'kv'), may hold values from -5 to 5
- values: bfloat16 [8192, 8, 128], P('srv', 'kv'), may hold values from -6 to 6
- lengths: int32 [16], replicated, may hold values from 1 to 1024, 8192 in all
- output_projection_weight: bfloat16 [8, 1024, 8192], P('kv', 'grp', 'srv'), may hold values from -0.0625 to 0.0625
Outputs:
- projected: bfloat16 [8192, 8192], P('srv', ('grp', 'kv'))
Inputs may be any that keep to these rules, and one draw needn't show every extreme that they name: The 16 lengths sum to 8192; the longest document has exactly 1024 tokens.
All inputs are finite; a program needn't handle non-finite values.
Results may differ from a plain program's by a relative error of at most 0.017.
Values may be sent and summed in bfloat16 or wider, within the bound.
No kernel may reach another device: no remote copies, remote signals or barrier semaphores. Data moves between devices by JAX's collectives and lax.ppermute only.
A program may use at most 64 MiB of HBM per device.

v0:
```python
import math
import jax
import jax.numpy as jnp
from jax import lax
from jax.sharding import PartitionSpec as P

REACH = 4


def from_behind(block, axis, distance):
    devices = range(lax.axis_size(axis))
    route = [(i - distance, i) for i in devices if i - distance in devices]
    return lax.ppermute(block, axis, route)


def sum_by_axis(array, axes, dim):
    if not axes:
        return array
    nearer = lax.psum_scatter(array, axes[0], scatter_dimension=dim, tiled=True)
    return sum_by_axis(nearer, axes[1:], dim)


def doc_starts(lengths, position):
    starts = jnp.cumsum(lengths) - lengths
    chosen = jnp.where(starts[None, :] <= position[:, None], starts[None, :], 0)
    return jnp.max(chosen, axis=1)


def attend(queries, window_keys, window_values, query_pos, key_pos, lengths):
    token_count = queries.shape[0]
    groups = queries.shape[1]
    head_size = window_keys.shape[2]
    heads = queries.shape[2] // head_size
    split_output = queries.reshape(token_count, groups, heads, head_size)
    scores = jnp.einsum(
        "tjhd,wjd->jhtw", split_output, window_keys, preferred_element_type=jnp.float32
    )
    scores = scores * (1.0 / math.sqrt(head_size))
    first_key = doc_starts(lengths, query_pos)
    allowed = (key_pos[None, :] >= first_key[:, None]) & (key_pos[None, :] <= query_pos[:, None])
    scores = jnp.where(allowed[None, None], scores, -jnp.inf)
    peak = jnp.max(scores, axis=3, keepdims=True)
    weights = jnp.exp(scores - peak)
    total = jnp.sum(weights, axis=3)
    numer = jnp.einsum(
        "jhtw,wjd->tjhd",
        weights.astype(jnp.bfloat16),
        window_values,
        preferred_element_type=jnp.float32,
    )
    final_output = numer / jnp.transpose(total, (2, 0, 1))[..., None]
    return final_output.astype(jnp.bfloat16).reshape(token_count, groups * heads * head_size)


def on_device(queries, keys, values, lengths, output_projection_weight):
    token_count = queries.shape[0]
    shard = lax.axis_index("srv")
    stacked = jnp.stack([keys, values])
    arrived = [stacked]
    for distance in range(1, REACH + 1):
        arrived.append(from_behind(stacked, "srv", distance))
    window = jnp.concatenate(arrived[::-1], axis=1)
    query_pos = shard * token_count + jnp.arange(token_count, dtype=jnp.int32)
    key_pos = (shard - REACH) * token_count + jnp.arange(window.shape[1], dtype=jnp.int32)
    attention_output = attend(queries, window[0], window[1], query_pos, key_pos, lengths)
    inner = attention_output.shape[1]
    piece = lax.all_gather(output_projection_weight, "srv", axis=2, tiled=True)
    partial_sum = jnp.dot(
        attention_output, piece.reshape(inner, piece.shape[2]), preferred_element_type=jnp.float32
    )
    summed = sum_by_axis(partial_sum.astype(jnp.bfloat16), ("grp", "kv"), 1).astype(jnp.float32)
    return summed.astype(jnp.bfloat16)


def solution(mesh):
    placed = (
        P("srv", "kv", "grp"),
        P("srv", "kv", None),
        P("srv", "kv", None),
        P(),
        P("kv", "grp", "srv"),
    )
    return jax.shard_map(
        on_device, mesh=mesh, in_specs=placed, out_specs=P("srv", ("grp", "kv")), check_vma=False
    )
```

profile of v0, /device:TPU:4, one launch (start us, length us, event | category | flops | bytes accessed | tf_op | source)
XLA Modules:
  0.0 212.5 jit_solution(3647171846262931791)
XLA Ops:
  6.5 0.0 all-gather.2.cloned.1.call-start
  6.5 0.7 all-gather.2.cloned.1.call-update
  7.3 0.0 reduce-scatter.3.cloned.1.call-start
  7.3 0.9 pad_maximum_fusion
  8.2 7.7 %collective-permute-start = (bf16[2,256,1,128]{3,1,2,0:T(8,128)(2,1)S(1)}, bf16[2,256,1,128]{3,1,2,0:T(8,128)(2,1)S(1)}, u32[]{:S(2)}, u32[]{:S(2)}) collective-permute-start(bf16[2,256,1,128]{3,1,2,0:T(8,128)(2,1)S(1)} %pad_maximum_fusion), channel_id=1, source_target_pairs={{0,4},{1,5},{2,6},{3,7},{4,8},{5,9},{6,10},{7,11},{8,12},{9,13},{1... | collective-permute-start | bytes 393224 | tf_op jit(solution)/shard_map/ppermute | solution.py:13
  15.9 2.8 %collective-permute-start.1 = (bf16[2,256,1,128]{3,1,2,0:T(8,128)(2,1)S(1)}, bf16[2,256,1,128]{3,1,2,0:T(8,128)(2,1)S(1)}, u32[]{:S(2)}, u32[]{:S(2)}) collective-permute-start(bf16[2,256,1,128]{3,1,2,0:T(8,128)(2,1)S(1)} %pad_maximum_fusion), channel_id=1, source_target_pairs={{0,3},{1,4},{2,5},{3,6},{4,7},{5,8},{6,9},{7,10},{8,11},{9,12},{10... | collective-permute-start | bytes 393224 | tf_op jit(solution)/shard_map/ppermute | solution.py:13
  18.8 3.3 %collective-permute-start.2 = (bf16[2,256,1,128]{3,1,2,0:T(8,128)(2,1)S(1)}, bf16[2,256,1,128]{3,1,2,0:T(8,128)(2,1)S(1)}, u32[]{:S(2)}, u32[]{:S(2)}) collective-permute-start(bf16[2,256,1,128]{3,1,2,0:T(8,128)(2,1)S(1)} %pad_maximum_fusion), channel_id=1, source_target_pairs={{0,2},{1,3},{2,4},{3,5},{4,6},{5,7},{6,8},{7,9},{8,10},{9,11},{10,... | collective-permute-start | bytes 393224 | tf_op jit(solution)/shard_map/ppermute | solution.py:13
  22.1 3.5 %collective-permute-start.3 = (bf16[2,256,1,128]{3,1,2,0:T(8,128)(2,1)S(1)}, bf16[2,256,1,128]{3,1,2,0:T(8,128)(2,1)S(1)}, u32[]{:S(2)}, u32[]{:S(2)}) collective-permute-start(bf16[2,256,1,128]{3,1,2,0:T(8,128)(2,1)S(1)} %pad_maximum_fusion), channel_id=1, source_target_pairs={{0,1},{1,2},{2,3},{3,4},{4,5},{5,6},{6,7},{7,8},{8,9},{9,10},{10,1... | collective-permute-start | bytes 393224 | tf_op jit(solution)/shard_map/ppermute | solution.py:13
  25.6 0.7 copy.14
  26.4 0.1 reduce.2
  26.5 0.7 sub.15
  27.1 0.1 select_reduce_fusion
  27.2 0.3 compare_and_fusion
  27.6 1.0 reshape.130
  28.6 0.0 collective-permute-done
  28.6 5.6 %collective-permute-done.1 = bf16[2,256,1,128]{3,1,2,0:T(8,128)(2,1)S(1)} collective-permute-done((bf16[2,256,1,128]{3,1,2,0:T(8,128)(2,1)S(1)}, bf16[2,256,1,128]{3,1,2,0:T(8,128)(2,1)S(1)}, u32[]{:S(2)}, u32[]{:S(2)}) %collective-permute-start.1) | collective-permute-done | bytes 131104 | tf_op jit(solution)/shard_map/ppermute | solution.py:13
  34.2 1.8 collective-permute-done.2
  36.1 5.3 %collective-permute-done.3 = bf16[2,256,1,128]{3,1,2,0:T(8,128)(2,1)S(1)} collective-permute-done((bf16[2,256,1,128]{3,1,2,0:T(8,128)(2,1)S(1)}, bf16[2,256,1,128]{3,1,2,0:T(8,128)(2,1)S(1)}, u32[]{:S(2)}, u32[]{:S(2)}) %collective-permute-start.3) | collective-permute-done | bytes 131104 | tf_op jit(solution)/shard_map/ppermute | solution.py:13
  41.4 0.9 constant_dynamic-update-slice_fusion
  42.3 1.0 fusion.17
  43.3 0.7 fusion.1
  44.0 1.0 fusion.13
  45.0 83.4 %all-gather.2.cloned.1.call-done = bf16[1,512,8192]{2,1,0:T(8,128)(2,1)} async-done(((bf16[1,512,256]{2,1,0:T(8,128)(2,1)}), bf16[1,512,8192]{2,1,0:T(8,128)(2,1)}) %all-gather.2.cloned.1.call-update) | async-done | bytes 8388624 | tf_op jit(solution)/shard_map/all_gather | solution.py:67
  128.4 7.7 %convolution_convert_fusion = bf16[256,8192]{1,0:T(8,128)(2,1)} fusion(bf16[256,512]{0,1:T(8,128)(2,1)S(1)} %bitcast.48, bf16[1,512,8192]{2,1,0:T(8,128)(2,1)} %all-gather.2.cloned.1.call-done), kind=kOutput, calls=%fused_computation | convolution fusion | flops 2149580800 | bytes 12845056 | tf_op jit(solution)/shard_map/dot_general | solution.py:68
  136.1 0.0 reduce-scatter.3.cloned.1.call-update
  136.1 0.0 reduce-scatter.5.cloned.1.call-start
  136.2 19.5 %reduce-scatter.3.cloned.1.call-done = bf16[256,4096]{1,0:T(8,128)(2,1)} async-done(((bf16[256,8192]{1,0:T(8,128)(2,1)}), bf16[256,4096]{1,0:T(8,128)(2,1)}) %reduce-scatter.3.cloned.1.call-update) | async-done | bytes 2097168 | tf_op jit(solution)/shard_map/reduce_scatter | solution.py:19
  155.7 0.0 reduce-scatter.5.cloned.1.call-update
  155.7 50.3 %reduce-scatter.5.cloned.1.call-done = bf16[256,512]{1,0:T(8,128)(2,1)} async-done(((bf16[256,4096]{1,0:T(8,128)(2,1)}), bf16[256,512]{1,0:T(8,128)(2,1)}) %reduce-scatter.5.cloned.1.call-update) | async-done | bytes 262160 | tf_op jit(solution)/shard_map/reduce_scatter | solution.py:19
  (7 shorter events, 0.1 us)
Async XLA Ops:
  6.5 121.9 %all-gather.2.cloned.1.call-start = ((), (), s32[]{:S(2)}) async-start(), calls=%async_computation.2 | async-start | bytes 8650752 | tf_op jit(solution)/shard_map/all_gather | solution.py:67
  7.3 148.4 %reduce-scatter.3.cloned.1.call-start = ((), (), s32[]{:S(2)}) async-start(), calls=%async_computation.3 | async-start | bytes 6291456 | tf_op jit(solution)/shard_map/reduce_scatter | solution.py:19
  8.2 20.4 %collective-permute-start = (bf16[2,256,1,128]{3,1,2,0:T(8,128)(2,1)S(1)}, bf16[2,256,1,128]{3,1,2,0:T(8,128)(2,1)S(1)}, u32[]{:S(2)}, u32[]{:S(2)}) collective-permute-start(bf16[2,256,1,128]{3,1,2,0:T(8,128)(2,1)S(1)} %pad_maximum_fusion), channel_id=1, source_target_pairs={{0,4},{1,5},{2,6},{3,7},{4,8},{5,9},{6,10},{7,11},{8,12},{9,13},{1... | collective-permute-start | bytes 393224 | tf_op jit(solution)/shard_map/ppermute | solution.py:13
  15.9 18.3 %collective-permute-start.1 = (bf16[2,256,1,128]{3,1,2,0:T(8,128)(2,1)S(1)}, bf16[2,256,1,128]{3,1,2,0:T(8,128)(2,1)S(1)}, u32[]{:S(2)}, u32[]{:S(2)}) collective-permute-start(bf16[2,256,1,128]{3,1,2,0:T(8,128)(2,1)S(1)} %pad_maximum_fusion), channel_id=1, source_target_pairs={{0,3},{1,4},{2,5},{3,6},{4,7},{5,8},{6,9},{7,10},{8,11},{9,12},{10... | collective-permute-start | bytes 393224 | tf_op jit(solution)/shard_map/ppermute | solution.py:13
  18.8 17.3 %collective-permute-start.2 = (bf16[2,256,1,128]{3,1,2,0:T(8,128)(2,1)S(1)}, bf16[2,256,1,128]{3,1,2,0:T(8,128)(2,1)S(1)}, u32[]{:S(2)}, u32[]{:S(2)}) collective-permute-start(bf16[2,256,1,128]{3,1,2,0:T(8,128)(2,1)S(1)} %pad_maximum_fusion), channel_id=1, source_target_pairs={{0,2},{1,3},{2,4},{3,5},{4,6},{5,7},{6,8},{7,9},{8,10},{9,11},{10,... | collective-permute-start | bytes 393224 | tf_op jit(solution)/shard_map/ppermute | solution.py:13
  22.1 19.3 %collective-permute-start.3 = (bf16[2,256,1,128]{3,1,2,0:T(8,128)(2,1)S(1)}, bf16[2,256,1,128]{3,1,2,0:T(8,128)(2,1)S(1)}, u32[]{:S(2)}, u32[]{:S(2)}) collective-permute-start(bf16[2,256,1,128]{3,1,2,0:T(8,128)(2,1)S(1)} %pad_maximum_fusion), channel_id=1, source_target_pairs={{0,1},{1,2},{2,3},{3,4},{4,5},{5,6},{6,7},{7,8},{8,9},{9,10},{10,1... | collective-permute-start | bytes 393224 | tf_op jit(solution)/shard_map/ppermute | solution.py:13
  136.1 69.8 %reduce-scatter.5.cloned.1.call-start = ((), (), s32[]{:S(2)}) async-start(), calls=%async_computation.4 | async-start | bytes 2359296 | tf_op jit(solution)/shard_map/reduce_scatter | solution.py:19
Sparse Core Ops, SparseCore 0:
  10.4 117.9 all-gather.1
  136.3 19.3 reduce-scatter.2
  158.8 47.1 reduce-scatter.4
where the time goes:
time: 213 us; the launch traced here: 212 us
  waiting for transfers between devices  167 us (78%)
  starting transfers between devices  17.4 us (8%)
  between operations  13.2 us (6%)
  matrix products  9.7 us (5%)
  other arithmetic  3.71 us (2%)
    all_gather x1, waiting for transfers between devices, on_device(): piece = lax.all_gather(output_projection_weight, 'srv', axis=2, tiled=True)  83.4 us
    reduce_scatter x2, waiting for transfers between devices, sum_by_axis(): nearer = lax.psum_scatter(array, axes[0], scatter_dimension=dim, tiled=True)  69.7 us
    ppermute x4, starting transfers between devices, from_behind(): return lax.ppermute(block, axis, route)  17.4 us
    ppermute x4, waiting for transfers between devices, from_behind(): return lax.ppermute(block, axis, route)  12.7 us
    dot_general x1, matrix products, on_device(): jnp.dot(attention_output, piece.reshape(inner, piece.shape[2]), preferred...  7.73 us
  transfers between devices with their start and end apart: 7, of which 6 were waited for; matrix products, arithmetic and copies ran while one was open for 4% of the time, Pallas kernels for 0%

commit v1 on v0

--- a/solution.py
+++ b/solution.py
@@ -5,6 +5,11 @@
 from jax.sharding import PartitionSpec as P
 
 REACH = 4
+
+
+def exchange_gather(block, mesh_axis, d):
+    sent = jnp.stack([block] * lax.axis_size(mesh_axis))
+    return jnp.concatenate(lax.all_to_all(sent, mesh_axis, 0, 0), axis=d)
 
 
 def from_behind(block, axis, distance):
@@ -64,7 +69,7 @@
     key_pos = (shard - REACH) * token_count + jnp.arange(window.shape[1], dtype=jnp.int32)
     attention_output = attend(queries, window[0], window[1], query_pos, key_pos, lengths)
     inner = attention_output.shape[1]
-    piece = lax.all_gather(output_projection_weight, "srv", axis=2, tiled=True)
+    piece = exchange_gather(output_projection_weight, "srv", 2)
     partial_sum = jnp.dot(
         attention_output, piece.reshape(inner, piece.shape[2]), preferred_element_type=jnp.float32
     )

time: 213 us -> 326 us (1.53)
  the two profiles are of different devices: /device:TPU:4 before, /device:TPU:6 now
where the time goes in v1:
time: 326 us
  waiting for transfers between devices  271 us (83%)
  starting transfers between devices  25 us (8%)
  between operations  13.6 us (4%)
  matrix products  9.76 us (3%)
  local copies, waits for them, and re-layouts  5.48 us (2%)
    ppermute x4, waiting for transfers between devices, from_behind(): return lax.ppermute(block, axis, route)  199 us
    reduce_scatter x2, waiting for transfers between devices, sum_by_axis(): nearer = lax.psum_scatter(array, axes[0], scatter_dimension=dim, tiled=True)  72.2 us
    ppermute x4, starting transfers between devices, from_behind(): return lax.ppermute(block, axis, route)  14.2 us
    all_to_all x1, starting transfers between devices, exchange_gather(): return jnp.concatenate(lax.all_to_all(sent, mesh_axis, 0, 0), axis=d)  10.7 us
    dot_general x1, matrix products, on_device(): jnp.dot(attention_output, piece.reshape(inner, piece.shape[2]), preferred...  7.77 us
  transfers between devices with their start and end apart: 7, of which 3 were waited for; matrix products, arithmetic and copies ran while one was open for 1% of the time, Pallas kernels for 0%

profile of v1, /device:TPU:6, one launch (start us, length us, event | category | flops | bytes accessed | tf_op | source)
XLA Modules:
  0.0 326.2 jit_solution(6398187930511812252)
XLA Ops:
  6.5 1.1 copy.25
  7.6 4.2 %stack.11 = bf16[32,1,512,256]{2,3,1,0:T(8,128)(2,1)} broadcast(bf16[512,256]{0,1:T(8,128)(2,1)S(1)} %copy.25), dimensions={2,3} | broadcast | bytes 8650752 | tf_op jit(solution)/shard_map/stack | solution.py:11
  11.8 0.0 copy-start.1
  11.8 0.0 copy-start.2
  11.8 0.0 copy-start.3
  11.8 0.0 copy-start
  11.8 10.7 %all-to-all-start = ((bf16[32,1,512,256]{2,3,1,0:T(8,128)(2,1)}), bf16[32,1,512,256]{2,3,1,0:T(8,128)(2,1)}, u32[]{:S(2)}, u32[]{:S(2)}) async-start(bf16[32,1,512,256]{2,3,1,0:T(8,128)(2,1)} %stack.11), calls=%async_computation | async-start | bytes 16777216 | tf_op jit(solution)/shard_map/all_to_all | solution.py:12
  22.5 0.0 reduce-scatter.3.cloned.1.call-start
  22.5 0.0 copy-done.1
  22.6 0.0 copy-done.2
  22.6 3.4 %collective-permute-start.3 = (bf16[2,256,1,128]{3,1,2,0:T(8,128)(2,1)S(1)}, bf16[2,256,1,128]{3,1,2,0:T(8,128)(2,1)S(1)}, u32[]{:S(2)}, u32[]{:S(2)}) collective-permute-start(bf16[2,256,1,128]{3,1,2,0:T(8,128)(2,1)S(1)} %pad_maximum_fusion), channel_id=1, source_target_pairs={{0,1},{1,2},{2,3},{3,4},{4,5},{5,6},{6,7},{7,8},{8,9},{9,10},{10,1... | collective-permute-start | bytes 393224 | tf_op jit(solution)/shard_map/ppermute | solution.py:18
  26.0 4.3 %collective-permute-start.2 = (bf16[2,256,1,128]{3,1,2,0:T(8,128)(2,1)S(1)}, bf16[2,256,1,128]{3,1,2,0:T(8,128)(2,1)S(1)}, u32[]{:S(2)}, u32[]{:S(2)}) collective-permute-start(bf16[2,256,1,128]{3,1,2,0:T(8,128)(2,1)S(1)} %pad_maximum_fusion), channel_id=1, source_target_pairs={{0,2},{1,3},{2,4},{3,5},{4,6},{5,7},{6,8},{7,9},{8,10},{9,11},{10,... | collective-permute-start | bytes 393224 | tf_op jit(solution)/shard_map/ppermute | solution.py:18
  30.3 4.6 %collective-permute-start.1 = (bf16[2,256,1,128]{3,1,2,0:T(8,128)(2,1)S(1)}, bf16[2,256,1,128]{3,1,2,0:T(8,128)(2,1)S(1)}, u32[]{:S(2)}, u32[]{:S(2)}) collective-permute-start(bf16[2,256,1,128]{3,1,2,0:T(8,128)(2,1)S(1)} %pad_maximum_fusion), channel_id=1, source_target_pairs={{0,3},{1,4},{2,5},{3,6},{4,7},{5,8},{6,9},{7,10},{8,11},{9,12},{10... | collective-permute-start | bytes 393224 | tf_op jit(solution)/shard_map/ppermute | solution.py:18
  34.9 1.9 collective-permute-start
  36.8 0.0 copy-done.3
  36.8 0.1 copy.21
  36.9 0.1 reduce.2
  37.1 0.1 select_reduce_fusion
  37.2 0.3 compare_and_fusion
  37.5 0.0 copy-done
  37.5 0.1 reshape.133
  37.6 198.8 %collective-permute-done = bf16[2,256,1,128]{3,1,2,0:T(8,128)(2,1)S(1)} collective-permute-done((bf16[2,256,1,128]{3,1,2,0:T(8,128)(2,1)S(1)}, bf16[2,256,1,128]{3,1,2,0:T(8,128)(2,1)S(1)}, u32[]{:S(2)}, u32[]{:S(2)}) %collective-permute-start) | collective-permute-done | bytes 131104 | tf_op jit(solution)/shard_map/ppermute | solution.py:18
  236.4 0.0 collective-permute-done.1
  236.5 0.0 collective-permute-done.2
  236.5 0.0 collective-permute-done.3
  236.6 1.0 fusion.16
  237.5 0.7 fusion
  238.2 1.0 fusion.12
  239.3 0.0 all-to-all-done
  239.3 7.8 %convolution_convert_fusion = bf16[256,8192]{1,0:T(8,128)(2,1)} fusion(bf16[256,512]{0,1:T(8,128)(2,1)S(1)} %bitcast.52, bf16[512,8192]{0,1:T(8,128)(2,1)} %bitcast.19), kind=kOutput, calls=%fused_computation | convolution fusion | flops 2149580800 | bytes 12845056 | tf_op jit(solution)/shard_map/dot_general | solution.py:73
  247.1 0.0 reduce-scatter.3.cloned.1.call-update
  247.1 0.0 reduce-scatter.5.cloned.1.call-start
  247.1 21.9 %reduce-scatter.3.cloned.1.call-done = bf16[256,4096]{1,0:T(8,128)(2,1)} async-done(((bf16[256,8192]{1,0:T(8,128)(2,1)}), bf16[256,4096]{1,0:T(8,128)(2,1)}) %reduce-scatter.3.cloned.1.call-update) | async-done | bytes 2097168 | tf_op jit(solution)/shard_map/reduce_scatter | solution.py:24
  269.1 0.0 reduce-scatter.5.cloned.1.call-update
  269.1 50.2 %reduce-scatter.5.cloned.1.call-done = bf16[256,512]{1,0:T(8,128)(2,1)} async-done(((bf16[256,4096]{1,0:T(8,128)(2,1)}), bf16[256,512]{1,0:T(8,128)(2,1)}) %reduce-scatter.5.cloned.1.call-update) | async-done | bytes 262160 | tf_op jit(solution)/shard_map/reduce_scatter | solution.py:24
  (10 shorter events, 0.2 us)
Async XLA Ops:
  11.8 10.8 %copy-start.1 = (bf16[256,1,128]{2,0,1:T(8,128)(2,1)S(1)}, bf16[256,1,128]{2,0,1:T(8,128)(2,1)}, u32[]{:S(2)}) copy-start(bf16[256,1,128]{2,0,1:T(8,128)(2,1)} %param.7) | copy-start | bytes 196612
  11.8 10.8 %copy-start.2 = (bf16[256,1,128]{2,0,1:T(8,128)(2,1)S(1)}, bf16[256,1,128]{2,0,1:T(8,128)(2,1)}, u32[]{:S(2)}) copy-start(bf16[256,1,128]{2,0,1:T(8,128)(2,1)} %param.6) | copy-start | bytes 196612
  11.8 25.0 %copy-start.3 = (s32[16]{0:T(128)S(1)}, s32[16]{0:T(128)}, u32[]{:S(2)}) copy-start(s32[16]{0:T(128)} %param.8) | copy-start | bytes 196
  11.8 25.7 %copy-start = (bf16[256,1,512]{2,0,1:T(8,128)(2,1)S(1)}, bf16[256,1,512]{2,0,1:T(8,128)(2,1)}, u32[]{:S(2)}) copy-start(bf16[256,1,512]{2,0,1:T(8,128)(2,1)} %param.5) | copy-start | bytes 786436
  11.8 227.5 %all-to-all-start = ((bf16[32,1,512,256]{2,3,1,0:T(8,128)(2,1)}), bf16[32,1,512,256]{2,3,1,0:T(8,128)(2,1)}, u32[]{:S(2)}, u32[]{:S(2)}) async-start(bf16[32,1,512,256]{2,3,1,0:T(8,128)(2,1)} %stack.11), calls=%async_computation | async-start | bytes 16777216 | tf_op jit(solution)/shard_map/all_to_all | solution.py:12
  22.5 246.6 %reduce-scatter.3.cloned.1.call-start = ((), (), s32[]{:S(2)}) async-start(), calls=%async_computation.3 | async-start | bytes 6291456 | tf_op jit(solution)/shard_map/reduce_scatter | solution.py:24
  22.6 213.9 %collective-permute-start.3 = (bf16[2,256,1,128]{3,1,2,0:T(8,128)(2,1)S(1)}, bf16[2,256,1,128]{3,1,2,0:T(8,128)(2,1)S(1)}, u32[]{:S(2)}, u32[]{:S(2)}) collective-permute-start(bf16[2,256,1,128]{3,1,2,0:T(8,128)(2,1)S(1)} %pad_maximum_fusion), channel_id=1, source_target_pairs={{0,1},{1,2},{2,3},{3,4},{4,5},{5,6},{6,7},{7,8},{8,9},{9,10},{10,1... | collective-permute-start | bytes 393224 | tf_op jit(solution)/shard_map/ppermute | solution.py:18
  26.0 210.5 %collective-permute-start.2 = (bf16[2,256,1,128]{3,1,2,0:T(8,128)(2,1)S(1)}, bf16[2,256,1,128]{3,1,2,0:T(8,128)(2,1)S(1)}, u32[]{:S(2)}, u32[]{:S(2)}) collective-permute-start(bf16[2,256,1,128]{3,1,2,0:T(8,128)(2,1)S(1)} %pad_maximum_fusion), channel_id=1, source_target_pairs={{0,2},{1,3},{2,4},{3,5},{4,6},{5,7},{6,8},{7,9},{8,10},{9,11},{10,... | collective-permute-start | bytes 393224 | tf_op jit(solution)/shard_map/ppermute | solution.py:18
  30.3 206.2 %collective-permute-start.1 = (bf16[2,256,1,128]{3,1,2,0:T(8,128)(2,1)S(1)}, bf16[2,256,1,128]{3,1,2,0:T(8,128)(2,1)S(1)}, u32[]{:S(2)}, u32[]{:S(2)}) collective-permute-start(bf16[2,256,1,128]{3,1,2,0:T(8,128)(2,1)S(1)} %pad_maximum_fusion), channel_id=1, source_target_pairs={{0,3},{1,4},{2,5},{3,6},{4,7},{5,8},{6,9},{7,10},{8,11},{9,12},{10... | collective-permute-start | bytes 393224 | tf_op jit(solution)/shard_map/ppermute | solution.py:18
  34.9 201.5 %collective-permute-start = (bf16[2,256,1,128]{3,1,2,0:T(8,128)(2,1)S(1)}, bf16[2,256,1,128]{3,1,2,0:T(8,128)(2,1)S(1)}, u32[]{:S(2)}, u32[]{:S(2)}) collective-permute-start(bf16[2,256,1,128]{3,1,2,0:T(8,128)(2,1)S(1)} %pad_maximum_fusion), channel_id=1, source_target_pairs={{0,4},{1,5},{2,6},{3,7},{4,8},{5,9},{6,10},{7,11},{8,12},{9,13},{1... | collective-permute-start | bytes 393224 | tf_op jit(solution)/shard_map/ppermute | solution.py:18
  247.1 72.2 %reduce-scatter.5.cloned.1.call-start = ((), (), s32[]{:S(2)}) async-start(), calls=%async_computation.4 | async-start | bytes 2359296 | tf_op jit(solution)/shard_map/reduce_scatter | solution.py:24
Sparse Core Ops, SparseCore 0:
  247.2 21.8 reduce-scatter.2
  272.2 47.1 reduce-scatter.4
